TPU v7x, 32 devices: a whole 2x2x4 slice. The times are simulated.
32 devices in a mesh: groups: 2 (over x), slot: 8 (over z, y), tensor: 2 (over core).
Axes of the slice: x: 2, y: 2, z: 4, core: 2. Of those that a mesh axis runs over, the one named last changes fastest.
Arguments:
- tokens: bfloat16 [1024, 3072], P(('groups', 'slot'), 'tensor'), parts along dimension 0, may hold values from -6 to 6
- expert_ids: int32 [1024, 2], P(('groups', 'slot')), parts along dimension 0, may hold values from 0 to 3, all different within a row; in each aligned block of 64 rows (0 to 63, 64 to 127, ...) at most 48 rows name the same one
- route_weights: float32 [1024, 2], P(('groups', 'slot')), parts along dimension 0, may hold values from 0.2 to 1
- up_weight: bfloat16 [8, 3072, 8192], P('slot', None, 'tensor'), as said below
- down_weight: bfloat16 [8, 8192, 3072], P('slot', 'tensor'), as said below
Outputs:
- mixed: bfloat16 [1024, 3072], P(('groups', 'slot'), 'tensor'), parts along dimension 0
There are 2 independent parts, one for each index of `groups`. A program takes and returns all parts, laid end to end along the dimension named above; an argument that names none is the same for every part. Nothing has to cross between parts.
Inputs may be any that keep to these rules, and one draw needn't show every extreme that they name: `expert_ids`: each row names 2 different experts; among the tokens of one slot index no expert is named by more than 48 rows, a bound that some expert reaches in some of these blocks. `up_weight`: the slices of copy 2 e + 1 hold the same numbers as those of copy 2 e. `down_weight`: the slices of copy 2 e + 1 hold the same numbers as those of copy 2 e.
All inputs are finite; a program needn't handle non-finite values.
Results may differ from a plain program's by a relative error of at most 0.005.
Values may be sent and summed in bfloat16 or wider, within the bound.
A program may use at most 128 MiB of HBM per device.

v0:
```python
import jax
import jax.numpy as jnp
from jax import lax
from jax.sharding import PartitionSpec as P

E = 4
CAP = 24


def shards(tokens, expert_ids, route_weights, up_weight, down_weight):
    slot_count = lax.axis_size("slot")
    tok_rows = tokens.shape[0]
    copy_count = 2 * E
    sub_count = slot_count // copy_count
    up_matrix = up_weight[0]
    down_matrix = down_weight[0]
    flat_ids = expert_ids.reshape(-1)
    one_hot = (flat_ids[:, None] == jnp.arange(E, dtype=jnp.int32)[None, :]).astype(jnp.int32)
    route_rank = jnp.sum(one_hot * (jnp.cumsum(one_hot, axis=0) - 1), axis=1)
    overflow = (route_rank >= CAP).astype(jnp.int32)
    target = ((2 * flat_ids + overflow) * CAP + route_rank - overflow * CAP).reshape(
        tok_rows, expert_ids.shape[1]
    )
    positions = jnp.arange(copy_count * CAP, dtype=jnp.int32)
    matches = target[None, :, :] == positions[:, None, None]
    chosen = jnp.sum(matches.astype(jnp.float32), axis=2).astype(jnp.bfloat16)
    scaled = jnp.sum(
        jnp.where(matches, route_weights[None, :, :], jnp.zeros_like(route_weights)[None, :, :]),
        axis=2,
    )
    gathered = lax.all_gather(tokens, "tensor", axis=1, tiled=True)
    packed = jnp.dot(chosen, gathered, preferred_element_type=jnp.float32).astype(jnp.bfloat16)
    feature_width = packed.shape[1]
    grouped = packed.reshape(copy_count, 1, CAP, feature_width)
    arrived = lax.all_to_all(
        jnp.broadcast_to(grouped, (copy_count, sub_count, CAP, feature_width)).reshape(
            slot_count, CAP, feature_width
        ),
        "slot",
        split_axis=0,
        concat_axis=0,
        tiled=True,
    )
    flat_rows = arrived.reshape(-1, arrived.shape[2])
    hidden = jax.nn.silu(jnp.dot(flat_rows, up_matrix, preferred_element_type=jnp.float32)).astype(
        jnp.bfloat16
    )
    result = jnp.dot(hidden, down_matrix, preferred_element_type=jnp.float32)
    partial_value = result.reshape(slot_count, arrived.shape[1], result.shape[1])
    returned = lax.all_to_all(partial_value, "slot", split_axis=0, concat_axis=0, tiled=True)
    feature_width = returned.shape[2]
    merged = jnp.sum(returned.reshape(copy_count, sub_count, CAP, feature_width), axis=1)
    merged = merged.reshape(copy_count * CAP, feature_width)
    mixed = lax.dot_general(
        scaled,
        merged,
        (((0,), (0,)), ((), ())),
        precision=lax.Precision.HIGHEST,
        preferred_element_type=jnp.float32,
    )
    mixed = lax.psum_scatter(mixed, "tensor", scatter_dimension=1, tiled=True)
    return mixed.astype(jnp.bfloat16)


def solution(mesh):
    return jax.shard_map(
        shards,
        mesh=mesh,
        in_specs=(
            P(("groups", "slot"), "tensor"),
            P(("groups", "slot"), None),
            P(("groups", "slot"), None),
            P("slot", None, "tensor"),
            P("slot", "tensor", None),
        ),
        out_specs=P(("groups", "slot"), "tensor"),
        check_vma=False,
    )
```

profile of v0, /device:TPU:0, one launch (start us, length us, event | category | flops | bytes accessed | tf_op | source)
XLA Modules:
  0.0 145.6 jit_solution(726951582053032262)
XLA Ops:
  6.5 0.0 reduce-scatter.2.cloned.1.call-start
  6.5 0.8 copy.24
  7.3 0.1 eq.28
  7.4 0.1 fusion.6
  7.5 0.2 reduce_window_sum.11
  7.7 0.2 select_reduce_fusion.1
  7.9 0.1 reduce_sum.34
  8.0 0.1 copy.25
  8.1 0.7 select_subtract_fusion
  8.8 2.4 %all_gather.3 = bf16[64,3072]{1,0:T(8,128)(2,1)S(1)} all-gather(bf16[64,1536]{1,0:T(8,128)(2,1)} %param.5), channel_id=1, replica_groups=mesh['groups'=2,'slot'=8,'tensor'=2] {'tensor'}, dimensions={1}, use_global_device_ids=true | all-gather | bytes 589824 | tf_op jit(solution)/shard_map/all_gather | solution.py:31
  11.2 0.8 convert_reduce_fusion
  12.0 0.5 convolution_convert_fusion
  12.5 36.2 %all_to_all.10 = bf16[8,24,3072]{2,1,0:T(8,128)(2,1)S(1)} all-to-all(bf16[8,24,3072]{2,1,0:T(8,128)(2,1)S(1)} %bitcast.20), channel_id=1, replica_groups=mesh['groups'=2,'slot'=8,'tensor'=2] {'slot'}, dimensions={0} | all-to-all | bytes 2359296 | tf_op jit(solution)/shard_map/all_to_all | solution.py:35
  48.7 10.9 %multiply_convert_fusion = bf16[192,4096]{1,0:T(8,128)(2,1)S(1)} fusion(bf16[192,3072]{1,0:T(8,128)(2,1)S(1)} %bitcast.21, bf16[1,3072,4096]{2,1,0:T(8,128)(2,1)} %param.8), kind=kOutput, calls=%fused_computation.5 | convolution fusion | flops 4835770368 | bytes 27918336 | tf_op jit(solution)/shard_map/dot_general | solution.py:45
  59.6 10.8 %fusion = f32[8,24,3072]{2,1,0:T(8,128)S(1)} fusion(bf16[8,24,4096]{2,1,0:T(8,128)(2,1)S(1)} %bitcast.22, bf16[1,4096,3072]{2,1,0:T(8,128)(2,1)} %param.9), kind=kOutput, calls=%fused_computation | convolution fusion | flops 4831838208 | bytes 29097984 | tf_op jit(solution)/shard_map/dot_general | solution.py:48
  70.5 56.8 %all_to_all.11 = f32[8,24,3072]{2,1,0:T(8,128)S(1)} all-to-all(f32[8,24,3072]{2,1,0:T(8,128)S(1)} %fusion), channel_id=1, replica_groups=mesh['groups'=2,'slot'=8,'tensor'=2] {'slot'}, dimensions={0} | all-to-all | bytes 4718592 | tf_op jit(solution)/shard_map/all_to_all | solution.py:50
  127.3 2.4 %fusion.8 = f32[64,3072]{1,0:T(8,128)} fusion(f32[192,64]{0,1:T(8,128)S(1)} %get-tuple-element.6, f32[192,3072]{1,0:T(8,128)S(1)} %bitcast.19), kind=kOutput, calls=%fused_computation.14 | convolution fusion | flops 452984832 | bytes 3194880 | tf_op jit(solution)/shard_map/dot_general | solution.py:54
  129.7 0.0 reduce-scatter.2.cloned.1.call-update
  129.8 7.3 %reduce-scatter.2.cloned.1.call-done = f32[64,1536]{1,0:T(8,128)} async-done(((f32[64,3072]{1,0:T(8,128)}), f32[64,1536]{1,0:T(8,128)}) %reduce-scatter.2.cloned.1.call-update) | async-done | bytes 393232 | tf_op jit(solution)/shard_map/reduce_scatter | solution.py:61
  137.1 1.7 %convert_element_type.29 = bf16[64,1536]{1,0:T(8,128)(2,1)} convert(f32[64,1536]{1,0:T(8,128)} %reduce-scatter.2.cloned.1.call-done) | non-fusion elementwise | flops 98304 | bytes 589824 | tf_op jit(solution)/shard_map/convert_element_type | solution.py:62
Async XLA Ops:
  6.5 130.6 %reduce-scatter.2.cloned.1.call-start = ((), (), s32[]{:S(2)}) async-start(), calls=%async_computation.3 | async-start | bytes 1179648 | tf_op jit(solution)/shard_map/reduce_scatter | solution.py:61
Sparse Core Ops, SparseCore 0:
  129.9 7.1 reduce-scatter.1
where the time goes:
time: 146 us
  blocking collectives  95.4 us (65%)
  matrix products  24.7 us (17%)
  between operations  13.4 us (9%)
  waiting for transfers between devices  7.35 us (5%)
  other arithmetic  3.61 us (2%)
    all_to_all x1, blocking collectives, shards(): lax.all_to_all(partial_value, 'slot', split_axis=0, concat_axis=0, tiled=...  56.8 us
    all_to_all x1, blocking collectives, shards(): lax.all_to_all(jnp.broadcast_to(grouped, (copy_count, sub_count, CAP, fea...  36.2 us
    dot_general x1, matrix products, shards(): jnp.dot(flat_rows, up_matrix, preferred_element_type=jnp.float32)  10.9 us
    dot_general x1, matrix products, shards(): result = jnp.dot(hidden, down_matrix, preferred_element_type=jnp.float32)  10.8 us
    reduce_scatter x1, waiting for transfers between devices, shards(): mixed = lax.psum_scatter(mixed, 'tensor', scatter_dimension=1, tiled=True)  7.33 us
  transfers between devices with their start and end apart: 1, of which 1 were waited for; matrix products, arithmetic and copies ran while one was open for 0% of the time, Pallas kernels for 0%

commit v1 on v0

--- a/solution.py
+++ b/solution.py
@@ -1,10 +1,272 @@
+import functools
+
 import jax
 import jax.numpy as jnp
 from jax import lax
+from jax.experimental import pallas as pl
+from jax.experimental.pallas import tpu as pltpu
 from jax.sharding import PartitionSpec as P
 
 E = 4
 CAP = 24
+MOST = 48
+WIDTH = 256
+UP_SLOTS = 4
+UP_TILE = 512
+MESH = pl.DeviceIdType.MESH
+
+
+def fused_kernel(
+    tok_ref, ids_ref, weight_ref, up_hbm, down_hbm, out_ref,
+    packed, x_own, x_sib, up_buf, down_buf, acc, hid, part_out, part_own, part_in, summed, returned,
+    up_sem, down_sem, go_send, go_recv, fwd_send, fwd_recv, part_send, part_recv, back_send, back_recv,
+):
+    tok_rows, half = tok_ref.shape
+    chunks = half // WIDTH
+    rows = E * MOST
+    hidden_units = acc.shape[1]
+    slot = lax.axis_index("slot")
+    core = lax.axis_index("tensor")
+    mine = slot // 2
+    lane = lax.rem(slot, 2)
+    sibling = 1 - core
+
+    def up_copies(c):
+        place = lax.rem(c, UP_SLOTS)
+        return [
+            pltpu.make_async_copy(
+                up_hbm.at[0, pl.ds(pl.multiple_of(side * half + c * WIDTH, WIDTH), WIDTH), :],
+                up_buf.at[place, i],
+                up_sem.at[place, i],
+            )
+            for i, side in enumerate((core, sibling))
+        ]
+
+    def down_copies(c):
+        return [
+            pltpu.make_async_copy(
+                down_hbm.at[0, :, pl.ds(pl.multiple_of(side * half + c * WIDTH, WIDTH), WIDTH)],
+                down_buf.at[c, i],
+                down_sem.at[c, i],
+            )
+            for i, side in enumerate((sibling, core))
+        ]
+
+    def peer(k):
+        return lax.rem(mine + k, E)
+
+    def go_copy(c, k):
+        return pltpu.make_async_remote_copy(
+            src_ref=packed.at[c, peer(k)],
+            dst_ref=x_own.at[c, mine],
+            send_sem=go_send.at[c, k - 1],
+            recv_sem=go_recv.at[c, k - 1],
+            device_id={"slot": peer(k) * 2 + lane},
+            device_id_type=MESH,
+        )
+
+    def fwd_copy(c):
+        return pltpu.make_async_remote_copy(
+            src_ref=x_own.at[c],
+            dst_ref=x_sib.at[c],
+            send_sem=fwd_send.at[c],
+            recv_sem=fwd_recv.at[c],
+            device_id={"tensor": sibling},
+            device_id_type=MESH,
+        )
+
+    def part_copy(c):
+        return pltpu.make_async_remote_copy(
+            src_ref=part_out.at[c],
+            dst_ref=part_in.at[c],
+            send_sem=part_send.at[c],
+            recv_sem=part_recv.at[c],
+            device_id={"tensor": sibling},
+            device_id_type=MESH,
+        )
+
+    def back_copy(c, k):
+        return pltpu.make_async_remote_copy(
+            src_ref=summed.at[c, peer(k)],
+            dst_ref=returned.at[c, mine],
+            send_sem=back_send.at[c, k - 1],
+            recv_sem=back_recv.at[c, k - 1],
+            device_id={"slot": peer(k) * 2 + lane},
+            device_id_type=MESH,
+        )
+
+    barrier = pltpu.get_barrier_semaphore()
+    for k in range(1, E):
+        pl.semaphore_signal(barrier, inc=1, device_id={"slot": peer(k) * 2 + lane}, device_id_type=MESH)
+    pl.semaphore_signal(barrier, inc=1, device_id={"tensor": sibling}, device_id_type=MESH)
+
+    for c in range(UP_SLOTS):
+        for copy in up_copies(c):
+            copy.start()
+
+    first, second = ids_ref[:, 0:1], ids_ref[:, 1:2]
+    experts = lax.broadcasted_iota(jnp.int32, (tok_rows, 128), 1)
+    is_first = jnp.where(experts == first, 1.0, 0.0)
+    is_second = jnp.where(experts == second, 1.0, 0.0)
+    before = jnp.where(
+        lax.broadcasted_iota(jnp.int32, (tok_rows, tok_rows), 0)
+        > lax.broadcasted_iota(jnp.int32, (tok_rows, tok_rows), 1),
+        1.0,
+        0.0,
+    ).astype(jnp.bfloat16)
+    rank = jnp.dot(before, (is_first + is_second).astype(jnp.bfloat16), preferred_element_type=jnp.float32)
+    place = rank + (experts * MOST).astype(jnp.float32)
+    columns = lax.broadcasted_iota(jnp.int32, (tok_rows, rows), 1).astype(jnp.float32)
+    one_first = jnp.where(columns == jnp.sum(is_first * place, axis=1, keepdims=True), 1.0, 0.0)
+    one_second = jnp.where(columns == jnp.sum(is_second * place, axis=1, keepdims=True), 1.0, 0.0)
+    chosen = (one_first + one_second).T.astype(jnp.bfloat16)
+    one_first = one_first.astype(jnp.bfloat16)
+    one_second = one_second.astype(jnp.bfloat16)
+
+    for c in range(chunks):
+        piece = jnp.dot(
+            chosen, tok_ref[:, c * WIDTH : (c + 1) * WIDTH], preferred_element_type=jnp.float32
+        ).astype(jnp.bfloat16)
+        packed[c] = piece.reshape(E, MOST, WIDTH)
+    pl.semaphore_wait(barrier, E)
+    for c in range(chunks):
+        for k in range(1, E):
+            go_copy(c, k).start()
+    for c in range(chunks):
+        x_own[c, mine] = packed[c, mine]
+
+    def up_step(c, start, final):
+        fwd_copy(c).wait_recv()
+        for copy in up_copies(c):
+            copy.wait()
+        spot = lax.rem(c, UP_SLOTS)
+        left = x_own[c].reshape(rows, WIDTH)
+        right = x_sib[c].reshape(rows, WIDTH)
+
+        @pl.loop(0, hidden_units // UP_TILE)
+        def _(n):
+            at = pl.ds(pl.multiple_of(n * UP_TILE, UP_TILE), UP_TILE)
+            value = jnp.dot(left, up_buf[spot, 0, :, at], preferred_element_type=jnp.float32)
+            value += jnp.dot(right, up_buf[spot, 1, :, at], preferred_element_type=jnp.float32)
+            if not start:
+                value += acc[:, at]
+            if final:
+                hid[:, at] = (value / (1.0 + jnp.exp(-value))).astype(jnp.bfloat16)
+            else:
+                acc[:, at] = value
+
+        for copy in down_copies(c):
+            copy.start()
+
+    def arrive(c):
+        for k in range(1, E):
+            go_copy(c, k).wait_recv()
+        fwd_copy(c).start()
+
+    arrive(0)
+    arrive(1)
+    up_step(0, True, False)
+    for copy in up_copies(UP_SLOTS):
+        copy.start()
+
+    @pl.loop(1, chunks - 1)
+    def _(c):
+        arrive(c + 1)
+        up_step(c, False, False)
+
+        @pl.when(c + UP_SLOTS < chunks)
+        def _():
+            for copy in up_copies(c + UP_SLOTS):
+                copy.start()
+
+    up_step(chunks - 1, False, True)
+
+    def finish(c):
+        part_copy(c).wait_recv()
+        total = (part_own[c] + part_in[c]).astype(jnp.bfloat16)
+        summed[c] = total.reshape(E, MOST, WIDTH)
+        for k in range(1, E):
+            back_copy(c, k).start()
+        returned[c, mine] = summed[c, mine]
+
+    @pl.loop(0, chunks)
+    def _(c):
+        for copy in down_copies(c):
+            copy.wait()
+        part_out[c] = jnp.dot(hid[...], down_buf[c, 0], preferred_element_type=jnp.float32)
+        part_copy(c).start()
+        part_own[c] = jnp.dot(hid[...], down_buf[c, 1], preferred_element_type=jnp.float32)
+
+        @pl.when(c > 0)
+        def _():
+            finish(c - 1)
+
+    finish(chunks - 1)
+
+    for c in range(chunks):
+        for k in range(1, E):
+            back_copy(c, k).wait_recv()
+        block = returned[c].reshape(rows, WIDTH)
+        value = weight_ref[:, 0:1] * jnp.dot(one_first, block, preferred_element_type=jnp.float32)
+        value += weight_ref[:, 1:2] * jnp.dot(one_second, block, preferred_element_type=jnp.float32)
+        out_ref[:, c * WIDTH : (c + 1) * WIDTH] = value.astype(jnp.bfloat16)
+
+    for c in range(chunks):
+        fwd_copy(c).wait_send()
+        part_copy(c).wait_send()
+        for k in range(1, E):
+            go_copy(c, k).wait_send()
+            back_copy(c, k).wait_send()
+
+
+def fused(tokens, expert_ids, route_weights, up_weight, down_weight):
+    tok_rows, half = tokens.shape
+    hidden_units = up_weight.shape[2]
+    chunks = half // WIDTH
+    rows = E * MOST
+    vmem = pl.BlockSpec(memory_space=pltpu.VMEM)
+    hbm = pl.BlockSpec(memory_space=pl.ANY)
+    sems = lambda *shape: pltpu.SemaphoreType.DMA(shape)
+    blocks = pltpu.VMEM((chunks, E, MOST, WIDTH), jnp.bfloat16)
+    wide = pltpu.VMEM((chunks, rows, WIDTH), jnp.float32)
+    return pl.pallas_call(
+        fused_kernel,
+        out_shape=jax.ShapeDtypeStruct((tok_rows, half), jnp.bfloat16),
+        in_specs=[vmem, vmem, vmem, hbm, hbm],
+        out_specs=vmem,
+        scratch_shapes=[
+            blocks,
+            blocks,
+            blocks,
+            pltpu.VMEM((UP_SLOTS, 2, WIDTH, hidden_units), jnp.bfloat16),
+            pltpu.VMEM((chunks, 2, hidden_units, WIDTH), jnp.bfloat16),
+            pltpu.VMEM((rows, hidden_units), jnp.float32),
+            pltpu.VMEM((rows, hidden_units), jnp.bfloat16),
+            wide,
+            wide,
+            wide,
+            blocks,
+            blocks,
+            sems(UP_SLOTS, 2),
+            sems(chunks, 2),
+            sems(chunks, E - 1),
+            sems(chunks, E - 1),
+            sems(chunks),
+            sems(chunks),
+            sems(chunks),
+            sems(chunks),
+            sems(chunks, E - 1),
+            sems(chunks, E - 1),
+        ],
+        compiler_params=pltpu.CompilerParams(
+            collective_id=0, has_side_effects=True, vmem_limit_bytes=60 * 1024 * 1024
+        ),
+        cost_estimate=pl.CostEstimate(
+            flops=8 * rows * half * hidden_units,
+            bytes_accessed=8 * half * hidden_units,
+            transcendentals=rows * hidden_units,
+        ),
+    )(tokens, expert_ids, route_weights, up_weight, down_weight)
 
 
 def shards(tokens, expert_ids, route_weights, up_weight, down_weight):
@@ -63,8 +325,9 @@
 
 
 def solution(mesh):
+    body = fused if mesh.shape["slot"] == 2 * E else shards
     return jax.shard_map(
-        shards,
+        body,
         mesh=mesh,
         in_specs=(
             P(("groups", "slot"), "tensor"),

time: 146 us -> 52.9 us (0.36)
  blocking collectives: 95.4 us -> 0 us
  Pallas kernels: 0 us -> 48.3 us
  matrix products: 24.7 us -> 0 us
  between operations: 13.4 us -> 0.01 us
  waiting for transfers between devices: 7.35 us -> 0 us
  other arithmetic: 3.61 us -> 0 us
  local copies, waits for them, and re-layouts: 1.11 us -> 4.36 us
    all_to_all x2 -> x0, blocking collectives: 93 us -> none  [the longest x1 56.8 us: shards(): lax.all_to_all(partial_value, 'slot', split_axis=0, concat_axis=0, tiled=...]
    pallas_call x0 -> x1, Pallas kernels: none -> 48.3 us  [fused(): pl.pallas_call(fused_kernel, out_shape=jax.ShapeDtypeStruct((tok_rows, ha...]
    dot_general x4 -> x0, matrix products: 24.7 us -> none  [the longest x1 10.9 us: shards(): jnp.dot(flat_rows, up_matrix, preferred_element_type=jnp.float32)]
    reduce_scatter x1 -> x0, waiting for transfers between devices: 7.33 us -> none  [shards(): mixed = lax.psum_scatter(mixed, 'tensor', scatter_dimension=1, tiled=True)]
    unnamed x1 -> x3, local copies, waits for them, and re-layouts: 0.77 us -> 4.36 us
    all_gather x1 -> x0, blocking collectives: 2.4 us -> none  [shards(): gathered = lax.all_gather(tokens, 'tensor', axis=1, tiled=True)]
    convert_element_type x2 -> x0, other arithmetic: 1.78 us -> none  [the longest x1 1.69 us: shards(): return mixed.astype(jnp.bfloat16)]
  transfers between devices with their start and end apart: 1 -> 0, of which waited for: 1 -> 0; matrix products, arithmetic and copies ran while one was open for 0% -> 0% of each run, Pallas kernels for 0% -> 0%
where the time goes in v1:
time: 52.9 us; the launch traced here: 52.7 us
  Pallas kernels  48.3 us (91%)
  local copies, waits for them, and re-layouts  4.36 us (8%)
    pallas_call x1, Pallas kernels, fused(): pl.pallas_call(fused_kernel, out_shape=jax.ShapeDtypeStruct((tok_rows, ha...  48.3 us
    unnamed x3, local copies, waits for them, and re-layouts  4.36 us

profile of v1, /device:TPU:0, one launch (start us, length us, event | category | flops | bytes accessed | tf_op | source)
XLA Modules:
  0.0 52.7 jit_solution(5052129245586696640)
XLA Ops:
  0.0 1.4 %copy.6.ids_ref = s32[64,2]{1,0:T(8,128)} copy(s32[64,2]{0,1:T(2,128)} %param.6) | data formatting | bytes 1024 | tf_op args[1]
  1.4 1.4 %copy.7.weight_ref = f32[64,2]{1,0:T(8,128)} copy(f32[64,2]{0,1:T(2,128)} %param.7) | data formatting | bytes 1024 | tf_op args[2]
  2.7 48.3 %shard_map.55 = bf16[64,1536]{1,0:T(8,128)(2,1)} custom-call(bf16[64,1536]{1,0:T(8,128)(2,1)} %tok_ref.1, s32[64,2]{1,0:T(8,128)} %copy.6.ids_ref, f32[64,2]{1,0:T(8,128)} %copy.7.weight_ref, bf16[1,3072,4096]{2,1,0:T(8,128)(2,1)} %up_hbm.1, bf16[1,4096,3072]{2,1,0:T(8,128)(2,1)} %down_hbm.1), custom_call_target="tpu_custom_call" | custom-call | flops 9663676416 | bytes 50331648 | tf_op jit(solution)/shard_map/pallas_call | solution.py:232
  51.0 1.6 %copy.9 = bf16[64,1536]{1,0:T(8,128)(2,1)} copy(bf16[64,1536]{1,0:T(8,128)(2,1)} %shard_map.55) | data formatting | bytes 393216

commit v2 on v1

--- a/solution.py
+++ b/solution.py
@@ -12,13 +12,14 @@
 MOST = 48
 WIDTH = 256
 UP_SLOTS = 4
-UP_TILE = 512
+UP_TILE = 2048
 MESH = pl.DeviceIdType.MESH
 
 
 def fused_kernel(
     tok_ref, ids_ref, weight_ref, up_hbm, down_hbm, out_ref,
     packed, x_own, x_sib, up_buf, down_buf, acc, hid, part_out, part_own, part_in, summed, returned,
+    turned_first, turned_second, gates,
     up_sem, down_sem, go_send, go_recv, fwd_send, fwd_recv, part_send, part_recv, back_send, back_recv,
 ):
     tok_rows, half = tok_ref.shape
@@ -104,82 +105,93 @@
         for copy in up_copies(c):
             copy.start()
 
-    first, second = ids_ref[:, 0:1], ids_ref[:, 1:2]
-    experts = lax.broadcasted_iota(jnp.int32, (tok_rows, 128), 1)
+    first, second = ids_ref[0:1, :], ids_ref[1:2, :]
+    experts = lax.broadcasted_iota(jnp.int32, (2 * E, tok_rows), 0)
     is_first = jnp.where(experts == first, 1.0, 0.0)
     is_second = jnp.where(experts == second, 1.0, 0.0)
     before = jnp.where(
         lax.broadcasted_iota(jnp.int32, (tok_rows, tok_rows), 0)
-        > lax.broadcasted_iota(jnp.int32, (tok_rows, tok_rows), 1),
+        < lax.broadcasted_iota(jnp.int32, (tok_rows, tok_rows), 1),
         1.0,
         0.0,
     ).astype(jnp.bfloat16)
-    rank = jnp.dot(before, (is_first + is_second).astype(jnp.bfloat16), preferred_element_type=jnp.float32)
+    rank = jnp.dot((is_first + is_second).astype(jnp.bfloat16), before, preferred_element_type=jnp.float32)
     place = rank + (experts * MOST).astype(jnp.float32)
-    columns = lax.broadcasted_iota(jnp.int32, (tok_rows, rows), 1).astype(jnp.float32)
-    one_first = jnp.where(columns == jnp.sum(is_first * place, axis=1, keepdims=True), 1.0, 0.0)
-    one_second = jnp.where(columns == jnp.sum(is_second * place, axis=1, keepdims=True), 1.0, 0.0)
-    chosen = (one_first + one_second).T.astype(jnp.bfloat16)
-    one_first = one_first.astype(jnp.bfloat16)
-    one_second = one_second.astype(jnp.bfloat16)
+    places = lax.broadcasted_iota(jnp.int32, (rows, tok_rows), 0).astype(jnp.float32)
+    one_first = jnp.where(places == jnp.sum(is_first * place, axis=0, keepdims=True), 1.0, 0.0)
+    one_second = jnp.where(places == jnp.sum(is_second * place, axis=0, keepdims=True), 1.0, 0.0)
+    chosen = (one_first + one_second).astype(jnp.bfloat16)
 
     for c in range(chunks):
         piece = jnp.dot(
             chosen, tok_ref[:, c * WIDTH : (c + 1) * WIDTH], preferred_element_type=jnp.float32
         ).astype(jnp.bfloat16)
         packed[c] = piece.reshape(E, MOST, WIDTH)
-    pl.semaphore_wait(barrier, E)
-    for c in range(chunks):
+        if c == 0:
+            pl.semaphore_wait(barrier, E)
         for k in range(1, E):
             go_copy(c, k).start()
     for c in range(chunks):
         x_own[c, mine] = packed[c, mine]
 
-    def up_step(c, start, final):
-        fwd_copy(c).wait_recv()
-        for copy in up_copies(c):
-            copy.wait()
-        spot = lax.rem(c, UP_SLOTS)
-        left = x_own[c].reshape(rows, WIDTH)
-        right = x_sib[c].reshape(rows, WIDTH)
+    turned_first[...] = one_first.T.astype(jnp.bfloat16)
+    turned_second[...] = one_second.T.astype(jnp.bfloat16)
+    gates[0] = jnp.broadcast_to(weight_ref[0:1, :], (128, tok_rows)).T
+    gates[1] = jnp.broadcast_to(weight_ref[1:2, :], (128, tok_rows)).T
+
+    def arrive(c):
+        for k in range(1, E):
+            go_copy(c, k).wait_recv()
+        fwd_copy(c).start()
+
+    def up_step(c, own, other):
+        if own:
+            up_copies(c)[0].wait()
+            left = x_own[c].reshape(rows, WIDTH)
+            spot = lax.rem(c, UP_SLOTS)
+        if other:
+            fwd_copy(c - 1).wait_recv()
+            up_copies(c - 1)[1].wait()
+            right = x_sib[c - 1].reshape(rows, WIDTH)
+            last = lax.rem(c - 1, UP_SLOTS)
 
         @pl.loop(0, hidden_units // UP_TILE)
         def _(n):
             at = pl.ds(pl.multiple_of(n * UP_TILE, UP_TILE), UP_TILE)
-            value = jnp.dot(left, up_buf[spot, 0, :, at], preferred_element_type=jnp.float32)
-            value += jnp.dot(right, up_buf[spot, 1, :, at], preferred_element_type=jnp.float32)
-            if not start:
+            value = None
+            if own:
+                value = jnp.dot(left, up_buf[spot, 0, :, at], preferred_element_type=jnp.float32)
+            if other:
+                more = jnp.dot(right, up_buf[last, 1, :, at], preferred_element_type=jnp.float32)
+                value = more if value is None else value + more
                 value += acc[:, at]
-            if final:
+            if own:
+                acc[:, at] = value
+            else:
                 hid[:, at] = (value / (1.0 + jnp.exp(-value))).astype(jnp.bfloat16)
-            else:
-                acc[:, at] = value
-
-        for copy in down_copies(c):
-            copy.start()
-
-    def arrive(c):
-        for k in range(1, E):
-            go_copy(c, k).wait_recv()
-        fwd_copy(c).start()
+
+        if own:
+            for copy in down_copies(c):
+                copy.start()
 
     arrive(0)
-    arrive(1)
     up_step(0, True, False)
-    for copy in up_copies(UP_SLOTS):
-        copy.start()
-
-    @pl.loop(1, chunks - 1)
+    up_copies(UP_SLOTS)[0].start()
+
+    @pl.loop(1, chunks)
     def _(c):
-        arrive(c + 1)
-        up_step(c, False, False)
+        arrive(c)
+        up_step(c, True, True)
 
         @pl.when(c + UP_SLOTS < chunks)
         def _():
-            for copy in up_copies(c + UP_SLOTS):
-                copy.start()
-
-    up_step(chunks - 1, False, True)
+            up_copies(c + UP_SLOTS)[0].start()
+
+        @pl.when(c - 1 + UP_SLOTS < chunks)
+        def _():
+            up_copies(c - 1 + UP_SLOTS)[1].start()
+
+    up_step(chunks, False, True)
 
     def finish(c):
         part_copy(c).wait_recv()
@@ -195,20 +207,21 @@
             copy.wait()
         part_out[c] = jnp.dot(hid[...], down_buf[c, 0], preferred_element_type=jnp.float32)
         part_copy(c).start()
-        part_own[c] = jnp.dot(hid[...], down_buf[c, 1], preferred_element_type=jnp.float32)
 
         @pl.when(c > 0)
         def _():
             finish(c - 1)
 
+        part_own[c] = jnp.dot(hid[...], down_buf[c, 1], preferred_element_type=jnp.float32)
+
     finish(chunks - 1)
 
     for c in range(chunks):
         for k in range(1, E):
             back_copy(c, k).wait_recv()
         block = returned[c].reshape(rows, WIDTH)
-        value = weight_ref[:, 0:1] * jnp.dot(one_first, block, preferred_element_type=jnp.float32)
-        value += weight_ref[:, 1:2] * jnp.dot(one_second, block, preferred_element_type=jnp.float32)
+        value = gates[0, :, 0:1] * jnp.dot(turned_first[...], block, preferred_element_type=jnp.float32)
+        value += gates[1, :, 0:1] * jnp.dot(turned_second[...], block, preferred_element_type=jnp.float32)
         out_ref[:, c * WIDTH : (c + 1) * WIDTH] = value.astype(jnp.bfloat16)
 
     for c in range(chunks):
@@ -247,6 +260,9 @@
             wide,
             blocks,
             blocks,
+            pltpu.VMEM((tok_rows, rows), jnp.bfloat16),
+            pltpu.VMEM((tok_rows, rows), jnp.bfloat16),
+            pltpu.VMEM((2, tok_rows, 128), jnp.float32),
             sems(UP_SLOTS, 2),
             sems(chunks, 2),
             sems(chunks, E - 1),
@@ -266,7 +282,7 @@
             bytes_accessed=8 * half * hidden_units,
             transcendentals=rows * hidden_units,
         ),
-    )(tokens, expert_ids, route_weights, up_weight, down_weight)
+    )(tokens, expert_ids.T, route_weights.T, up_weight, down_weight)
 
 
 def shards(tokens, expert_ids, route_weights, up_weight, down_weight):

time: 52.9 us -> 44.7 us (0.84)
  Pallas kernels: 48.3 us -> 42.9 us
  local copies, waits for them, and re-layouts: 4.36 us -> 1.62 us
    pallas_call x1, Pallas kernels: 48.3 us -> 42.9 us  [fused(): pl.pallas_call(fused_kernel, out_shape=jax.ShapeDtypeStruct((tok_rows, ha...]
    unnamed x3 -> x1, local copies, waits for them, and re-layouts: 4.36 us -> 1.62 us
where the time goes in v2:
time: 44.7 us; the launch traced here: 44.6 us
  Pallas kernels  42.9 us (96%)
  local copies, waits for them, and re-layouts  1.62 us (4%)
    pallas_call x1, Pallas kernels, fused(): pl.pallas_call(fused_kernel, out_shape=jax.ShapeDtypeStruct((tok_rows, ha...  42.9 us
    unnamed x1, local copies, waits for them, and re-layouts  1.62 us

profile of v2, /device:TPU:0, one launch (start us, length us, event | category | flops | bytes accessed | tf_op | source)
XLA Modules:
  0.0 44.6 jit_solution(7579376758144860722)
XLA Ops:
  0.0 42.9 %shard_map.55 = bf16[64,1536]{1,0:T(8,128)(2,1)} custom-call(bf16[64,1536]{1,0:T(8,128)(2,1)} %tok_ref.1, s32[2,64]{1,0:T(2,128)} %bitcast.2, f32[2,64]{1,0:T(2,128)} %bitcast.3, bf16[1,3072,4096]{2,1,0:T(8,128)(2,1)} %up_hbm.1, bf16[1,4096,3072]{2,1,0:T(8,128)(2,1)} %down_hbm.1), custom_call_target="tpu_custom_call" | custom-call | flops 9663676416 | bytes 50331648 | tf_op jit(solution)/shard_map/pallas_call | solution.py:245
  43.0 1.6 %copy.7 = bf16[64,1536]{1,0:T(8,128)(2,1)} copy(bf16[64,1536]{1,0:T(8,128)(2,1)} %shard_map.55) | data formatting | bytes 393216

commit v3 on v2

--- a/solution.py
+++ b/solution.py
@@ -12,7 +12,7 @@
 MOST = 48
 WIDTH = 256
 UP_SLOTS = 4
-UP_TILE = 2048
+UP_TILE = 4096
 MESH = pl.DeviceIdType.MESH
 
 

time: 44.7 us -> 44 us (0.984)
  Pallas kernels: 42.9 us -> 42.2 us
    pallas_call x1, Pallas kernels: 42.9 us -> 42.2 us  [fused(): pl.pallas_call(fused_kernel, out_shape=jax.ShapeDtypeStruct((tok_rows, ha...]
where the time goes in v3:
time: 44 us; the launch traced here: 43.8 us
  Pallas kernels  42.2 us (96%)
  local copies, waits for them, and re-layouts  1.62 us (4%)
    pallas_call x1, Pallas kernels, fused(): pl.pallas_call(fused_kernel, out_shape=jax.ShapeDtypeStruct((tok_rows, ha...  42.2 us
    unnamed x1, local copies, waits for them, and re-layouts  1.62 us

profile of v3, /device:TPU:0, one launch (start us, length us, event | category | flops | bytes accessed | tf_op | source)
XLA Modules:
  0.0 43.8 jit_solution(11669832716630204587)
XLA Ops:
  0.0 42.2 %shard_map.55 = bf16[64,1536]{1,0:T(8,128)(2,1)} custom-call(bf16[64,1536]{1,0:T(8,128)(2,1)} %tok_ref.1, s32[2,64]{1,0:T(2,128)} %bitcast.2, f32[2,64]{1,0:T(2,128)} %bitcast.3, bf16[1,3072,4096]{2,1,0:T(8,128)(2,1)} %up_hbm.1, bf16[1,4096,3072]{2,1,0:T(8,128)(2,1)} %down_hbm.1), custom_call_target="tpu_custom_call" | custom-call | flops 9663676416 | bytes 50331648 | tf_op jit(solution)/shard_map/pallas_call | solution.py:245
  42.2 1.6 %copy.7 = bf16[64,1536]{1,0:T(8,128)(2,1)} copy(bf16[64,1536]{1,0:T(8,128)(2,1)} %shard_map.55) | data formatting | bytes 393216
